TPU v7x, 32 devices: a whole 2x2x4 slice. The times are simulated.
32 devices in a mesh: dp: 8 (over z, x), tensor: 4 (over y, core).
Axes of the slice: x: 2, y: 2, z: 4, core: 2. Of those that a mesh axis runs over, the one named last changes fastest.
Arguments:
- hidden_in: bfloat16 [16384, 640], P('dp'), may hold values from -6 to 6
- query_weight: bfloat16 [640, 1024], P(None, 'tensor'), may hold values from -0.25 to 0.25
- key_weight: bfloat16 [640, 256], replicated, may hold values from -0.25 to 0.25
- value_weight: bfloat16 [640, 256], replicated, may hold values from -0.25 to 0.25
- output_weight: bfloat16 [1024, 640], P('tensor'), may hold values from -0.1875 to 0.1875
- gate_weight: bfloat16 [640, 2048], P(None, 'tensor'), may hold values from -0.25 to 0.25
- up_weight: bfloat16 [640, 2048], P(None, 'tensor'), may hold values from -0.25 to 0.25
- down_weight: bfloat16 [2048, 640], P('tensor'), may hold values from -0.125 to 0.125
- pre_attention: float32 [640], replicated, may hold values from -0.5 to 0.5
- query_norm: float32 [256], replicated, may hold values from -0.5 to 0.5
- key_norm: float32 [256], replicated, may hold values from -0.5 to 0.5
- post_attention: float32 [640], replicated, may hold values from -0.5 to 0.5
- pre_feedforward: float32 [640], replicated, may hold values from -0.5 to 0.5
- post_feedforward: float32 [640], replicated, may hold values from -0.5 to 0.5
- segments: int32 [16384], P('dp'), may hold values from 0 to 15, as said below
- positions: int32 [16384], P('dp'), may hold values from 0 to 511, as said below
- cotangent: bfloat16 [16384, 640], P('dp'), may hold values from -6 to 6
Outputs:
- hidden_out: bfloat16 [16384, 640], P('dp')
- grad_input: float32 [16384, 640], P('dp')
- grad_query_weight: float32 [640, 1024], P(None, 'tensor')
- grad_key_weight: float32 [640, 256], replicated
- grad_value_weight: float32 [640, 256], replicated
- grad_output_weight: float32 [1024, 640], P('tensor')
- grad_gate_weight: float32 [640, 2048], P(None, 'tensor')
- grad_up_weight: float32 [640, 2048], P(None, 'tensor')
- grad_down_weight: float32 [2048, 640], P('tensor')
- grad_pre_attention: float32 [640], replicated
- grad_query_norm: float32 [256], replicated
- grad_key_norm: float32 [256], replicated
- grad_post_attention: float32 [640], replicated
- grad_pre_feedforward: float32 [640], replicated
- grad_post_feedforward: float32 [640], replicated
Inputs may be any that keep to these rules, and one draw needn't show every extreme that they name: `segments`: within each aligned block of 512 tokens the document numbers start at 0 at the block's first token and rise by 0 or 1 from one token to the next. `positions`: each token's position is its distance from the first token of its document in the same block.
All inputs are finite; a program needn't handle non-finite values.
Results may differ from a plain program's by a relative error of at most 0.02.
Values may be sent and summed in bfloat16 or wider, within the bound.
A program may use at most 128 MiB of HBM per device.

v0:
```python
import jax
import jax.numpy as jnp
from jax import lax
from jax.sharding import PartitionSpec as P

LEN = 512
epsilon = 1e-06
rope_base = 1000000.0
masked_score = -1e30


def normed(values, norm_gain):
    inverse = lax.rsqrt(jnp.mean(values * values, axis=-1, keepdims=True) + epsilon)
    return values * inverse * (1.0 + norm_gain)


def rotary(values, cosine, sine_table):
    half_width = values.shape[-1] // 2
    front_half = values[..., :half_width]
    second = values[..., half_width:]
    return jnp.concatenate(
        [front_half * cosine - second * sine_table, second * cosine + front_half * sine_table],
        axis=-1,
    )


def rotary_tables(positions, head_width):
    steps_half = jnp.arange(head_width // 2).astype(jnp.float32)
    frequency = jnp.power(jnp.float32(rope_base), -2.0 * steps_half / head_width)
    angles = positions.astype(jnp.float32)[:, None] * frequency[None, :]
    return (jnp.cos(angles), jnp.sin(angles))


def gated(gate_proj, up_proj):
    return jax.nn.gelu(gate_proj, approximate=True) * up_proj


def pack_mask(segment):
    offsets = jnp.arange(segment.shape[0])
    return (segment[:, None] == segment[None, :]) & (offsets[None, :] <= offsets[:, None])


def pack_scores(queries, key_rows, segment):
    score_scale = queries.shape[-1] ** (-0.5)
    scores = (
        jnp.einsum("ihd,jd->hij", queries, key_rows, preferred_element_type=jnp.float32)
        * score_scale
    )
    return jnp.where(pack_mask(segment)[None], scores, masked_score)


def attend_pack(inputs):
    queries, key_rows, values, segment = inputs
    scores = pack_scores(queries, key_rows, segment)
    top_score = jnp.max(scores, axis=-1, keepdims=True)
    log_total = top_score + jnp.log(jnp.sum(jnp.exp(scores - top_score), axis=-1, keepdims=True))
    prob_low = jnp.exp(scores - log_total).astype(jnp.bfloat16)
    mixture = jnp.einsum("hij,jd->ihd", prob_low, values, preferred_element_type=jnp.float32)
    return (mixture.astype(jnp.bfloat16), log_total)


def attend_back(inputs):
    queries, key_rows, values, segment, log_total, mixture_grad = inputs
    score_scale = queries.shape[-1] ** (-0.5)
    probability = jnp.exp(pack_scores(queries, key_rows, segment) - log_total)
    prob_low = probability.astype(jnp.bfloat16)
    value_grad = jnp.einsum(
        "hij,ihd->jhd", prob_low, mixture_grad, preferred_element_type=jnp.float32
    )
    prob_grad = jnp.einsum("ihd,jd->hij", mixture_grad, values, preferred_element_type=jnp.float32)
    row_terms = jnp.sum(probability * prob_grad, axis=-1, keepdims=True)
    score_grad = (probability * (prob_grad - row_terms)).astype(jnp.bfloat16)
    query_grad = (
        jnp.einsum("hij,jd->ihd", score_grad, key_rows, preferred_element_type=jnp.float32)
        * score_scale
    )
    key_grad = (
        jnp.einsum("hij,ihd->jhd", score_grad, queries, preferred_element_type=jnp.float32)
        * score_scale
    )
    return (query_grad, key_grad, value_grad.astype(jnp.bfloat16))


def run_layer(
    hidden_in,
    query_weight,
    key_weight,
    value_weight,
    output_weight,
    gate_weight,
    up_weight,
    down_weight,
    pre_attention,
    query_norm,
    key_norm,
    post_attention,
    pre_feedforward,
    post_feedforward,
    segments,
    positions,
    cotangent,
    reducers,
    feed_hook,
):
    attention_reduce, feed_reduce, feed_back_reduce, attention_back_reduce = reducers
    tokens = hidden_in.shape[0]
    pack_length = LEN
    pack_count = tokens // pack_length
    head_width = key_weight.shape[1]
    local_heads = query_weight.shape[1] // head_width
    hidden = hidden_in.astype(jnp.float32)
    cosine, sine_table = rotary_tables(positions, head_width)

    def head_path(projected, norm_gain):
        return rotary(normed(projected, norm_gain), cosine[:, None, :], sine_table[:, None, :])

    normed_value, pre_back = jax.vjp(normed, hidden, pre_attention)
    normed_in = normed_value.astype(jnp.bfloat16)
    query_proj = jnp.dot(normed_in, query_weight, preferred_element_type=jnp.float32)
    query_proj = query_proj.reshape(tokens, local_heads, head_width)
    key_proj = jnp.dot(normed_in, key_weight, preferred_element_type=jnp.float32)
    value_low = jnp.dot(normed_in, value_weight, preferred_element_type=jnp.float32).astype(
        jnp.bfloat16
    )
    query_rot, query_back = jax.vjp(head_path, query_proj, query_norm)
    key_heads = key_proj[:, None, :]
    key_rot, key_back = jax.vjp(head_path, key_heads, key_norm)
    query_packs = query_rot.astype(jnp.bfloat16).reshape(
        pack_count, pack_length, local_heads, head_width
    )
    key_packs = key_rot[:, 0, :].astype(jnp.bfloat16).reshape(pack_count, pack_length, head_width)
    value_packs = value_low.reshape(pack_count, pack_length, head_width)
    segment_packs = segments.reshape(pack_count, pack_length)
    mixture, log_total = lax.map(attend_pack, (query_packs, key_packs, value_packs, segment_packs))
    mixture_low = mixture.reshape(tokens, local_heads * head_width)
    attention = attention_reduce(
        jnp.dot(mixture_low, output_weight, preferred_element_type=jnp.float32)
    )
    post_value, post_att_back = jax.vjp(normed, attention, post_attention)
    middle = hidden + post_value
    mid_value, mid_back = jax.vjp(normed, middle, pre_feedforward)
    normed_mid = mid_value.astype(jnp.bfloat16)
    gate_proj = jnp.dot(normed_mid, gate_weight, preferred_element_type=jnp.float32)
    up_proj = jnp.dot(normed_mid, up_weight, preferred_element_type=jnp.float32)
    product, gated_back = jax.vjp(gated, gate_proj, up_proj)
    product_low = product.astype(jnp.bfloat16)
    feed = feed_reduce(jnp.dot(product_low, down_weight, preferred_element_type=jnp.float32))
    feed_value, feed_out_back = jax.vjp(normed, feed, post_feedforward)
    hidden_out = (middle + feed_value).astype(jnp.bfloat16)
    cotangent_full = cotangent.astype(jnp.float32)
    feed_grad, grad_post_feedforward = feed_out_back(cotangent_full)
    feed_grad_low = feed_grad.astype(jnp.bfloat16)
    grad_down_weight = jnp.einsum(
        "tf,td->fd", product_low, feed_grad_low, preferred_element_type=jnp.float32
    )
    product_grad = jnp.einsum(
        "td,fd->tf", feed_grad_low, down_weight, preferred_element_type=jnp.float32
    )
    gate_grad, up_grad = gated_back(product_grad)
    gate_grad_low = gate_grad.astype(jnp.bfloat16)
    up_grad_low = up_grad.astype(jnp.bfloat16)
    grad_gate_weight = jnp.einsum(
        "td,tf->df", normed_mid, gate_grad_low, preferred_element_type=jnp.float32
    )
    grad_up_weight = jnp.einsum(
        "td,tf->df", normed_mid, up_grad_low, preferred_element_type=jnp.float32
    )
    grad_gate_weight, grad_up_weight, grad_down_weight, grad_post_feedforward = feed_hook(
        (grad_gate_weight, grad_up_weight, grad_down_weight, grad_post_feedforward)
    )
    mid_part = jnp.einsum(
        "tf,df->td", gate_grad_low, gate_weight, preferred_element_type=jnp.float32
    )
    mid_part = mid_part + jnp.einsum(
        "tf,df->td", up_grad_low, up_weight, preferred_element_type=jnp.float32
    )
    mid_normed_grad = feed_back_reduce(mid_part)
    middle_part, grad_pre_feedforward = mid_back(mid_normed_grad)
    middle_grad = cotangent_full + middle_part
    attention_grad, grad_post_attention = post_att_back(middle_grad)
    attention_grad_low = attention_grad.astype(jnp.bfloat16)
    grad_output_weight = jnp.einsum(
        "tk,td->kd", mixture_low, attention_grad_low, preferred_element_type=jnp.float32
    )
    mixture_grad = jnp.einsum(
        "td,kd->tk", attention_grad_low, output_weight, preferred_element_type=jnp.float32
    )
    mixture_grad_packs = mixture_grad.astype(jnp.bfloat16).reshape(
        pack_count, pack_length, local_heads, head_width
    )
    query_rot_grad, key_rot_grad, value_grad_low = lax.map(
        attend_back,
        (query_packs, key_packs, value_packs, segment_packs, log_total, mixture_grad_packs),
    )
    query_grad, grad_query_norm = query_back(
        query_rot_grad.reshape(tokens, local_heads, head_width)
    )
    key_grad, grad_key_norm = key_back(key_rot_grad.reshape(tokens, local_heads, head_width))
    query_grad_low = query_grad.astype(jnp.bfloat16).reshape(tokens, local_heads * head_width)
    key_grad_low = key_grad.astype(jnp.bfloat16)
    value_grad_low = value_grad_low.reshape(tokens, local_heads, head_width)
    grad_query_weight = jnp.einsum(
        "td,tk->dk", normed_in, query_grad_low, preferred_element_type=jnp.float32
    )
    grad_key_weight = jnp.einsum(
        "td,thk->dk", normed_in, key_grad_low, preferred_element_type=jnp.float32
    )
    grad_value_weight = jnp.einsum(
        "td,thk->dk", normed_in, value_grad_low, preferred_element_type=jnp.float32
    )
    in_part = jnp.einsum(
        "tk,dk->td", query_grad_low, query_weight, preferred_element_type=jnp.float32
    )
    in_part = in_part + jnp.einsum(
        "thk,dk->td", key_grad_low, key_weight, preferred_element_type=jnp.float32
    )
    in_part = in_part + jnp.einsum(
        "thk,dk->td", value_grad_low, value_weight, preferred_element_type=jnp.float32
    )
    in_normed_grad = attention_back_reduce(in_part)
    input_part, grad_pre_attention = pre_back(in_normed_grad)
    grad_input = middle_grad + input_part
    return (
        hidden_out,
        grad_input,
        grad_query_weight,
        grad_key_weight,
        grad_value_weight,
        grad_output_weight,
        grad_gate_weight,
        grad_up_weight,
        grad_down_weight,
        grad_pre_attention,
        grad_query_norm,
        grad_key_norm,
        grad_post_attention,
        grad_pre_feedforward,
        grad_post_feedforward,
    )


def on_device(
    hidden_in,
    query_weight,
    key_weight,
    value_weight,
    output_weight,
    gate_weight,
    up_weight,
    down_weight,
    pre_attention,
    query_norm,
    key_norm,
    post_attention,
    pre_feedforward,
    post_feedforward,
    segments,
    positions,
    cotangent,
):

    def attention_reduce(values):
        return lax.psum(values, "tensor")

    def feed_reduce(values):
        return lax.psum(values.astype(jnp.bfloat16), "tensor").astype(jnp.float32)

    def feed_back_reduce(values):
        return lax.psum(values.astype(jnp.bfloat16), "tensor").astype(jnp.float32)

    def attention_back_reduce(values):
        return lax.psum(values.astype(jnp.bfloat16), "tensor").astype(jnp.float32)

    def feed_hook(grads):
        return grads

    (
        hidden_out,
        grad_input,
        grad_query_weight,
        grad_key_weight,
        grad_value_weight,
        grad_output_weight,
        grad_gate_weight,
        grad_up_weight,
        grad_down_weight,
        grad_pre_attention,
        grad_query_norm,
        grad_key_norm,
        grad_post_attention,
        grad_pre_feedforward,
        grad_post_feedforward,
    ) = run_layer(
        hidden_in,
        query_weight,
        key_weight,
        value_weight,
        output_weight,
        gate_weight,
        up_weight,
        down_weight,
        pre_attention,
        query_norm,
        key_norm,
        post_attention,
        pre_feedforward,
        post_feedforward,
        segments,
        positions,
        cotangent,
        (attention_reduce, feed_reduce, feed_back_reduce, attention_back_reduce),
        feed_hook,
    )
    grad_key_weight, grad_value_weight, grad_query_norm, grad_key_norm = lax.psum(
        (grad_key_weight, grad_value_weight, grad_query_norm, grad_key_norm), ("dp", "tensor")
    )
    (
        grad_query_weight,
        grad_output_weight,
        grad_gate_weight,
        grad_up_weight,
        grad_down_weight,
        grad_pre_attention,
        grad_post_attention,
        grad_pre_feedforward,
        grad_post_feedforward,
    ) = lax.psum(
        (
            grad_query_weight,
            grad_output_weight,
            grad_gate_weight,
            grad_up_weight,
            grad_down_weight,
            grad_pre_attention,
            grad_post_attention,
            grad_pre_feedforward,
            grad_post_feedforward,
        ),
        "dp",
    )
    return (
        hidden_out,
        grad_input,
        grad_query_weight,
        grad_key_weight,
        grad_value_weight,
        grad_output_weight,
        grad_gate_weight,
        grad_up_weight,
        grad_down_weight,
        grad_pre_attention,
        grad_query_norm,
        grad_key_norm,
        grad_post_attention,
        grad_pre_feedforward,
        grad_post_feedforward,
    )


def solution(mesh):
    placed = (
        P("dp", None),
        P(None, "tensor"),
        P(),
        P(),
        P("tensor", None),
        P(None, "tensor"),
        P(None, "tensor"),
        P("tensor", None),
        P(),
        P(),
        P(),
        P(),
        P(),
        P(),
        P("dp"),
        P("dp"),
        P("dp", None),
    )
    return jax.shard_map(
        on_device,
        mesh=mesh,
        in_specs=placed,
        out_specs=(
            P("dp", None),
            P("dp", None),
            P(None, "tensor"),
            P(),
            P(),
            P("tensor", None),
            P(None, "tensor"),
            P(None, "tensor"),
            P("tensor", None),
            P(),
            P(),
            P(),
            P(),
            P(),
            P(),
        ),
        check_vma=False,
    )
```

profile of v0, /device:TPU:0, one launch (start us, length us, event | category | flops | bytes accessed | tf_op | source)
XLA Modules:
  0.0 909.8 jit_solution(12823472843531258651)
XLA Ops:
  21.3 5.7 fusion.99
  35.6 3.7 convolution_convert_fusion.4
  43.3 26.9 %while.26 = (s32[]{:T(128)}, bf16[4,512,1,256]{3,1,0,2:T(8,128)(2,1)}, f32[4,1,512,1]{2,3,1,0:T(1,128)}, bf16[4,512,256]{2,1,0:T(8,128)(2,1)}, s32[4,512]{1,0:T(...) while((s32[]{:T(128)}, bf16[4,512,1,256]{3,1,0,2:T(8,128)(2,1)}, ...), condition=%wide.region_6.7_spmd, body=%wide.region_3.6_spmd.sunk | while | flops 271187456 | bytes 5272153 | solution.py:134
  70.2 4.6 fusion.115
  75.6 104.7 %all-reduce.15.cloned.1.call-done = f32[2048,640]{1,0:T(8,128)} async-done(((f32[2048,640]{1,0:T(8,128)}), f32[2048,640]{1,0:T(8,128)}) %all-reduce.15.cloned.1.call-update) | async-done | bytes 5242896 | tf_op jit(solution)/shard_map/psum | solution.py:263
  190.1 4.1 multiply_convert_fusion.3
  199.4 59.6 %all-reduce.17.cloned.1.call-done = bf16[2048,640]{1,0:T(8,128)(2,1)} async-done(((bf16[2048,640]{1,0:T(8,128)(2,1)}), bf16[2048,640]{1,0:T(8,128)(2,1)}) %all-reduce.17.cloned.1.call-update) | async-done | bytes 2621456 | tf_op jit(solution)/shard_map/psum | solution.py:266
  261.5 4.2 fusion.57
  267.9 4.9 multiply_convert_fusion.2
  278.4 5.3 fusion.126
  283.6 54.6 %all-reduce.19.cloned.1.call-done = bf16[2048,640]{1,0:T(8,128)(2,1)} async-done(((bf16[2048,640]{1,0:T(8,128)(2,1)}), bf16[2048,640]{1,0:T(8,128)(2,1)}) %all-reduce.19.cloned.1.call-update) | async-done | bytes 2621456 | tf_op jit(solution)/shard_map/psum | solution.py:269
  338.3 4.4 fusion.55
  343.1 7.7 multiply_reduce_fusion.1
  355.8 125.7 %while.27 = (s32[]{:T(128)}, f32[4,512,1,256]{1,0,3,2:T(4,128)}, f32[4,512,1,256]{1,0,3,2:T(4,128)}, bf16[4,512,1,256]{3,1,0,2:T(8,128)(2,1)}, bf16[4,512,256]{2...) while((s32[]{:T(128)}, f32[4,512,1,256]{1,0,3,2:T(4,128)}, ...), condition=%wide.region_18.19_spmd, body=%wide.region_16.18_spmd.sunk | while | flops 674627072 | bytes 16275081 | solution.py:191
  362.1 11.0 %dynamic_update_slice.30 = f32[4,512,1,256]{1,0,3,2:T(4,128)} dynamic-update-slice(f32[4,512,1,256]{1,0,3,2:T(4,128)} %get-tuple-element.387, f32[1,512,1,256]{1,0,3,2:T(1,128)S(1)} %copy.93, s32[]{:T(128)} %get-tuple-element.385, s32[]{:T(128)} %constant.83.clone.1..sunk, s32[]{:T(128)} %constant.83.clone.1..sunk, s32[]{:T(128)} %constant.83.clone.1..sunk) | dynamic-update-slice | bytes 1048580 | tf_op jit(solution)/shard_map/while/body/jit(dynamic_update_index_in_dim)/dynamic_update_slice | solution.py:191
  374.9 11.1 %dynamic_update_slice.29 = f32[4,512,1,256]{1,0,3,2:T(4,128)} dynamic-update-slice(f32[4,512,1,256]{1,0,3,2:T(4,128)} %get-tuple-element.386, f32[1,512,1,256]{1,0,3,2:T(1,128)S(1)} %copy.92, s32[]{:T(128)} %get-tuple-element.385, s32[]{:T(128)} %constant.83.clone.1..sunk, s32[]{:T(128)} %constant.83.clone.1..sunk, s32[]{:T(128)} %constant.83.clone.1..sunk) | dynamic-update-slice | bytes 1048580 | tf_op jit(solution)/shard_map/while/body/jit(dynamic_update_index_in_dim)/dynamic_update_slice | solution.py:191
  393.5 11.0 %dynamic_update_slice.30 = f32[4,512,1,256]{1,0,3,2:T(4,128)} dynamic-update-slice(f32[4,512,1,256]{1,0,3,2:T(4,128)} %get-tuple-element.387, f32[1,512,1,256]{1,0,3,2:T(1,128)S(1)} %copy.93, s32[]{:T(128)} %get-tuple-element.385, s32[]{:T(128)} %constant.83.clone.1..sunk, s32[]{:T(128)} %constant.83.clone.1..sunk, s32[]{:T(128)} %constant.83.clone.1..sunk) | dynamic-update-slice | bytes 1048580 | tf_op jit(solution)/shard_map/while/body/jit(dynamic_update_index_in_dim)/dynamic_update_slice | solution.py:191
  406.3 11.1 %dynamic_update_slice.29 = f32[4,512,1,256]{1,0,3,2:T(4,128)} dynamic-update-slice(f32[4,512,1,256]{1,0,3,2:T(4,128)} %get-tuple-element.386, f32[1,512,1,256]{1,0,3,2:T(1,128)S(1)} %copy.92, s32[]{:T(128)} %get-tuple-element.385, s32[]{:T(128)} %constant.83.clone.1..sunk, s32[]{:T(128)} %constant.83.clone.1..sunk, s32[]{:T(128)} %constant.83.clone.1..sunk) | dynamic-update-slice | bytes 1048580 | tf_op jit(solution)/shard_map/while/body/jit(dynamic_update_index_in_dim)/dynamic_update_slice | solution.py:191
  425.0 11.0 %dynamic_update_slice.30 = f32[4,512,1,256]{1,0,3,2:T(4,128)} dynamic-update-slice(f32[4,512,1,256]{1,0,3,2:T(4,128)} %get-tuple-element.387, f32[1,512,1,256]{1,0,3,2:T(1,128)S(1)} %copy.93, s32[]{:T(128)} %get-tuple-element.385, s32[]{:T(128)} %constant.83.clone.1..sunk, s32[]{:T(128)} %constant.83.clone.1..sunk, s32[]{:T(128)} %constant.83.clone.1..sunk) | dynamic-update-slice | bytes 1048580 | tf_op jit(solution)/shard_map/while/body/jit(dynamic_update_index_in_dim)/dynamic_update_slice | solution.py:191
  437.8 11.1 %dynamic_update_slice.29 = f32[4,512,1,256]{1,0,3,2:T(4,128)} dynamic-update-slice(f32[4,512,1,256]{1,0,3,2:T(4,128)} %get-tuple-element.386, f32[1,512,1,256]{1,0,3,2:T(1,128)S(1)} %copy.92, s32[]{:T(128)} %get-tuple-element.385, s32[]{:T(128)} %constant.83.clone.1..sunk, s32[]{:T(128)} %constant.83.clone.1..sunk, s32[]{:T(128)} %constant.83.clone.1..sunk) | dynamic-update-slice | bytes 1048580 | tf_op jit(solution)/shard_map/while/body/jit(dynamic_update_index_in_dim)/dynamic_update_slice | solution.py:191
  456.4 11.0 %dynamic_update_slice.30 = f32[4,512,1,256]{1,0,3,2:T(4,128)} dynamic-update-slice(f32[4,512,1,256]{1,0,3,2:T(4,128)} %get-tuple-element.387, f32[1,512,1,256]{1,0,3,2:T(1,128)S(1)} %copy.93, s32[]{:T(128)} %get-tuple-element.385, s32[]{:T(128)} %constant.83.clone.1..sunk, s32[]{:T(128)} %constant.83.clone.1..sunk, s32[]{:T(128)} %constant.83.clone.1..sunk) | dynamic-update-slice | bytes 1048580 | tf_op jit(solution)/shard_map/while/body/jit(dynamic_update_index_in_dim)/dynamic_update_slice | solution.py:191
  469.2 11.1 %dynamic_update_slice.29 = f32[4,512,1,256]{1,0,3,2:T(4,128)} dynamic-update-slice(f32[4,512,1,256]{1,0,3,2:T(4,128)} %get-tuple-element.386, f32[1,512,1,256]{1,0,3,2:T(1,128)S(1)} %copy.92, s32[]{:T(128)} %get-tuple-element.385, s32[]{:T(128)} %constant.83.clone.1..sunk, s32[]{:T(128)} %constant.83.clone.1..sunk, s32[]{:T(128)} %constant.83.clone.1..sunk) | dynamic-update-slice | bytes 1048580 | tf_op jit(solution)/shard_map/while/body/jit(dynamic_update_index_in_dim)/dynamic_update_slice | solution.py:191
  484.2 3.7 reshape.591
  487.9 7.3 fusion.104
  506.5 4.3 fusion.124
  517.0 4.1 fusion.123
  522.9 40.3 %all-reduce.4 = (f32[256]{0:T(256)}, f32[256]{0:T(256)}) all-reduce(f32[256]{0:T(256)S(1)} %get-tuple-element.156, f32[256]{0:T(256)S(1)} %get-tuple-element.154), channel_id=1, replica_groups=mesh['dp'=8,'tensor'=4] {'dp','tensor'}, use_global_device_ids=true, to_apply=%region_33.34 | all-reduce | flops 512 | bytes 4096 | tf_op jit(solution)/shard_map/psum | solution.py:314
  566.2 4.0 fusion.56
  570.2 37.7 %all-reduce.6 = (f32[640]{0:T(1024)}, f32[640]{0:T(1024)}, f32[640]{0:T(1024)}, f32[640]{0:T(1024)}) all-reduce(f32[640]{0:T(1024)S(1)} %get-tuple-element.152, f32[640]{0:T(1024)S(1)} %get-tuple-element.146, f32[640]{0:T(1024)S(1)} %get-tuple-element.148, f32[640]{0:T(1024)S(1)} %get-tuple-element.150), channel_id=1, replica_groups=mesh['dp'=8,'tensor'=4] {'dp'}, use_global_device_ids=true, to_apply=%region_31.32 | all-reduce | flops 2560 | bytes 20480 | tf_op jit(solution)/shard_map/psum | solution.py:327
  607.9 5.5 fusion.60
  613.4 90.6 %all-reduce.23.cloned.1.call-done = (f32[640,256]{1,0:T(8,128)}, f32[640,256]{1,0:T(8,128)}) async-done(((f32[640,256]{1,0:T(8,128)}, f32[640,256]{1,0:T(8,128)}), (f32[640,256]{1,0:T(8,128)}, f32[640,256]{1,0:T(8,128)})) %all-reduce.23.cloned.1.call-update) | async-done | bytes 1310736 | tf_op jit(solution)/shard_map/psum | solution.py:314
  704.0 189.8 %all-reduce.25.cloned.1.call-done = (f32[640,256]{1,0:T(8,128)}, f32[256,640]{1,0:T(8,128)}, f32[640,512]{1,0:T(8,128)}, f32[640,512]{1,0:T(8,128)}, f32[512,640]{1,0:T(8,128)}) async-done(((f32[640,256]{1,0:T(8,128)}, f32[256,640]{1,0:T(8,128)}, f32[640,512]{1,0:T(8,128)}, f32[640,512]{1,0:T(8,128)}, f32[512,640]{1,0:T(8,128)}), (f32[640,256]{1,0:T(8,128)}, f32[256,640]{1,0:T(8,128)}, ...) | async-done | bytes 5242896 | tf_op jit(solution)/shard_map/psum | solution.py:327
  (312 shorter events, 155.3 us)
Async XLA Ops:
  7.2 188.3 %copy-start = (bf16[512,640]{1,0:T(8,128)(2,1)S(1)}, bf16[512,640]{1,0:T(8,128)(2,1)}, u32[]{:S(2)}) copy-start(bf16[512,640]{1,0:T(8,128)(2,1)} %param.28) | copy-start | bytes 1966084
  7.2 173.1 %all-reduce.15.cloned.1.call-start = ((), (), s32[]{:S(2)}) async-start(), calls=%async_computation | async-start | bytes 10485760 | tf_op jit(solution)/shard_map/psum | solution.py:263
  7.3 14.0 %copy-start.66 = (f32[128]{0:T(128)}, f32[128]{0:T(128)S(1)}, u32[]{:S(2)}) copy-start(f32[128]{0:T(128)S(1)} %multiply_power_fusion) | copy-start | bytes 1540
  10.8 4.7 copy-start.15
  13.2 5.4 copy-start.46
  15.5 5.8 copy-start.54
  15.6 5.7 copy-start.44
  74.9 184.1 %all-reduce.17.cloned.1.call-start = ((), (), s32[]{:S(2)}) async-start(), calls=%async_computation.1 | async-start | bytes 5242880 | tf_op jit(solution)/shard_map/psum | solution.py:266
  190.1 4.1 copy-start.70
  198.8 139.5 %all-reduce.19.cloned.1.call-start = ((), (), s32[]{:S(2)}) async-start(), calls=%async_computation.2 | async-start | bytes 5242880 | tf_op jit(solution)/shard_map/psum | solution.py:269
  261.5 4.2 copy-start.12
  261.5 5.7 copy-start.73
  267.2 5.6 copy-start.27
  267.9 4.9 copy-start.37
  278.1 288.0 %all-reduce.21.cloned.1.call-start = ((), (), s32[]{:S(2)}) async-start(), calls=%async_computation.3 | async-start | bytes 5242880 | tf_op jit(solution)/shard_map/psum | solution.py:272
  338.3 4.4 copy-start.13
  338.3 4.8 copy-start.18
  342.7 8.2 slice-start
  343.1 7.8 slice-start.1
  487.9 7.4 copy-start.8
  487.9 7.4 copy-start.47
  487.9 7.4 copy-start.59
  504.8 199.2 %all-reduce.23.cloned.1.call-start = ((), (), s32[]{:S(2)}) async-start(), calls=%async_computation.4 | async-start | bytes 2621440 | tf_op jit(solution)/shard_map/psum | solution.py:314
  506.5 4.3 copy-start.20
  516.9 4.1 copy-start.17
  517.0 376.8 %all-reduce.25.cloned.1.call-start = ((), (), s32[]{:S(2)}) async-start(), calls=%async_computation.5 | async-start | bytes 10485760 | tf_op jit(solution)/shard_map/psum | solution.py:327
  517.0 4.1 copy-start.22
  522.8 43.3 %copy-start.5 = (bf16[2048,640]{1,0:T(8,128)(2,1)S(1)}, bf16[2048,640]{1,0:T(8,128)(2,1)}, u32[]{:S(2)}) copy-start(bf16[2048,640]{1,0:T(8,128)(2,1)} %param.21) | copy-start | bytes 7864324
  563.1 44.7 %copy-start.51 = (f32[2048]{0:T(1024)S(1)}, f32[2048]{0:T(1024)}, u32[]{:S(2)}) copy-start(f32[2048]{0:T(1024)} %copy-done.50) | copy-start | bytes 24580
  704.0 193.9 %copy-start.34 = (f32[640,256]{1,0:T(8,128)S(1)}, f32[640,256]{1,0:T(8,128)}, u32[]{:S(2)}) copy-start(f32[640,256]{1,0:T(8,128)} %get-tuple-element.413) | copy-start | bytes 1966084
  893.8 4.9 copy-start.35
  893.8 5.8 copy-start.33
  (50 other events, 104.7 us)
Sparse Core Ops, SparseCore 0:
  75.0 105.2 all-reduce.14
  198.9 60.0 all-reduce.16
  278.3 59.9 all-reduce.18
  504.9 61.2 all-reduce.20
  572.2 131.7 all-reduce.22
  709.3 184.4 all-reduce.24
where the time goes:
time: 920 us; the launch traced here: 910 us
  waiting for transfers between devices  502 us (55%)
  local copies, waits for them, and re-layouts  153 us (17%)
  matrix products  95.9 us (10%)
  blocking collectives  77.9 us (8%)
  other arithmetic  63.7 us (7%)
  between operations  15.2 us (2%)
    psum x1, waiting for transfers between devices, on_device(): lax.psum((grad_query_weight, grad_output_weight, grad_gate_weight, grad_u...  190 us
    psum x1, waiting for transfers between devices, attention_reduce(): return lax.psum(values, 'tensor')  105 us
    dynamic_update_slice x16, local copies, waits for them, and re-layouts, run_layer(): lax.map(attend_back, (query_packs, key_packs, value_packs, segment_packs,...  92.6 us
    psum x1, waiting for transfers between devices, on_device(): lax.psum((grad_key_weight, grad_value_weight, grad_query_norm, grad_key_n...  90.6 us
    psum x1, waiting for transfers between devices, feed_reduce(): return lax.psum(values.astype(jnp.bfloat16), 'tensor').astype(jnp.float32)  59.6 us
    psum x1, waiting for transfers between devices, feed_back_reduce(): return lax.psum(values.astype(jnp.bfloat16), 'tensor').astype(jnp.float32)  54.6 us
    psum x1, blocking collectives, on_device(): lax.psum((grad_key_weight, grad_value_weight, grad_query_norm, grad_key_n...  40.3 us
    psum x1, blocking collectives, on_device(): lax.psum((grad_query_weight, grad_output_weight, grad_gate_weight, grad_u...  37.7 us
  transfers between devices with their start and end apart: 6, of which 6 were waited for; matrix products, arithmetic and copies ran while one was open for 3% of the time, Pallas kernels for 0%

commit v1 on v0

--- a/solution.py
+++ b/solution.py
@@ -311,8 +311,11 @@
         (attention_reduce, feed_reduce, feed_back_reduce, attention_back_reduce),
         feed_hook,
     )
-    grad_key_weight, grad_value_weight, grad_query_norm, grad_key_norm = lax.psum(
-        (grad_key_weight, grad_value_weight, grad_query_norm, grad_key_norm), ("dp", "tensor")
+    map_ratios = lambda original, mesh_name, which_axis: lax.psum(
+        lax.psum(original, mesh_name), which_axis
+    )
+    grad_key_weight, grad_value_weight, grad_query_norm, grad_key_norm = map_ratios(
+        (grad_key_weight, grad_value_weight, grad_query_norm, grad_key_norm), "tensor", "dp"
     )
     (
         grad_query_weight,

time: 920 us -> 865 us (0.940)
  blocking collectives: 77.9 us -> 45.7 us
  waiting for transfers between devices: 502 us -> 478 us
    psum x1, waiting for transfers between devices: 90.6 us -> 20.4 us  [on_device(): lax.psum(original, mesh_name)]
    psum x1, waiting for transfers between devices: 3.04 us -> 56 us  [attention_back_reduce(): return lax.psum(values.astype(jnp.bfloat16), 'tensor').astype(jnp.float32)]
    psum x1, blocking collectives: 40.3 us -> 6.19 us  [on_device(): lax.psum(original, mesh_name)]
    unnamed x159 -> x157, local copies, waits for them, and re-layouts: 20.7 us -> 19.8 us
  transfers between devices with their start and end apart: 6 -> 6, of which waited for: 6 -> 6; matrix products, arithmetic and copies ran while one was open for 3% -> 4% of each run, Pallas kernels for 0% -> 0%
where the time goes in v1:
time: 865 us; the launch traced here: 855 us
  waiting for transfers between devices  478 us (55%)
  local copies, waits for them, and re-layouts  152 us (18%)
  matrix products  98.7 us (11%)
  other arithmetic  63.9 us (7%)
  blocking collectives  45.7 us (5%)
  between operations  15.2 us (2%)
    psum x1, waiting for transfers between devices, on_device(): lax.psum((grad_query_weight, grad_output_weight, grad_gate_weight, grad_u...  182 us
    psum x1, waiting for transfers between devices, attention_reduce(): return lax.psum(values, 'tensor')  105 us
    dynamic_update_slice x16, local copies, waits for them, and re-layouts, run_layer(): lax.map(attend_back, (query_packs, key_packs, value_packs, segment_packs,...  92.5 us
    psum x1, waiting for transfers between devices, feed_reduce(): return lax.psum(values.astype(jnp.bfloat16), 'tensor').astype(jnp.float32)  59.6 us
    psum x1, waiting for transfers between devices, attention_back_reduce(): return lax.psum(values.astype(jnp.bfloat16), 'tensor').astype(jnp.float32)  56 us
    psum x1, waiting for transfers between devices, feed_back_reduce(): return lax.psum(values.astype(jnp.bfloat16), 'tensor').astype(jnp.float32)  54.6 us
    psum x1, blocking collectives, on_device(): lax.psum((grad_query_weight, grad_output_weight, grad_gate_weight, grad_u...  39.5 us
    reduce_sum x6, other arithmetic, normed(): return values * inverse * (1.0 + norm_gain)  21.5 us
  transfers between devices with their start and end apart: 6, of which 6 were waited for; matrix products, arithmetic and copies ran while one was open for 4% of the time, Pallas kernels for 0%

profile of v1, /device:TPU:0, one launch (start us, length us, event | category | flops | bytes accessed | tf_op | source)
XLA Modules:
  0.0 854.7 jit_solution(2162961058803706571)
XLA Ops:
  21.4 5.7 fusion.99
  35.6 3.7 convolution_convert_fusion.4
  43.3 26.8 %while.26 = (s32[]{:T(128)}, bf16[4,512,1,256]{3,1,0,2:T(8,128)(2,1)}, f32[4,1,512,1]{2,3,1,0:T(1,128)}, bf16[4,512,256]{2,1,0:T(8,128)(2,1)}, s32[4,512]{1,0:T(...) while((s32[]{:T(128)}, bf16[4,512,1,256]{3,1,0,2:T(8,128)(2,1)}, ...), condition=%wide.region_6.7_spmd, body=%wide.region_3.6_spmd.sunk | while | flops 271187456 | bytes 5272153 | solution.py:134
  70.2 4.6 fusion.115
  75.5 104.7 %all-reduce.15.cloned.1.call-done = f32[2048,640]{1,0:T(8,128)} async-done(((f32[2048,640]{1,0:T(8,128)}), f32[2048,640]{1,0:T(8,128)}) %all-reduce.15.cloned.1.call-update) | async-done | bytes 5242896 | tf_op jit(solution)/shard_map/psum | solution.py:263
  190.0 4.1 multiply_convert_fusion.3
  199.4 59.6 %all-reduce.17.cloned.1.call-done = bf16[2048,640]{1,0:T(8,128)(2,1)} async-done(((bf16[2048,640]{1,0:T(8,128)(2,1)}), bf16[2048,640]{1,0:T(8,128)(2,1)}) %all-reduce.17.cloned.1.call-update) | async-done | bytes 2621456 | tf_op jit(solution)/shard_map/psum | solution.py:266
  261.5 4.2 fusion.57
  267.8 4.9 multiply_convert_fusion.2
  278.3 5.3 fusion.126
  283.6 54.6 %all-reduce.19.cloned.1.call-done = bf16[2048,640]{1,0:T(8,128)(2,1)} async-done(((bf16[2048,640]{1,0:T(8,128)(2,1)}), bf16[2048,640]{1,0:T(8,128)(2,1)}) %all-reduce.19.cloned.1.call-update) | async-done | bytes 2621456 | tf_op jit(solution)/shard_map/psum | solution.py:269
  338.2 4.4 fusion.55
  343.1 7.7 multiply_reduce_fusion.1
  355.7 125.6 %while.27 = (s32[]{:T(128)}, f32[4,512,1,256]{1,0,3,2:T(4,128)}, f32[4,512,1,256]{1,0,3,2:T(4,128)}, bf16[4,512,1,256]{3,1,0,2:T(8,128)(2,1)}, bf16[4,512,256]{2...) while((s32[]{:T(128)}, f32[4,512,1,256]{1,0,3,2:T(4,128)}, ...), condition=%wide.region_18.19_spmd, body=%wide.region_16.18_spmd.sunk | while | flops 674627072 | bytes 16275081 | solution.py:191
  362.0 11.0 %dynamic_update_slice.30 = f32[4,512,1,256]{1,0,3,2:T(4,128)} dynamic-update-slice(f32[4,512,1,256]{1,0,3,2:T(4,128)} %get-tuple-element.391, f32[1,512,1,256]{1,0,3,2:T(1,128)S(1)} %copy.93, s32[]{:T(128)} %get-tuple-element.389, s32[]{:T(128)} %constant.83.clone.1..sunk, s32[]{:T(128)} %constant.83.clone.1..sunk, s32[]{:T(128)} %constant.83.clone.1..sunk) | dynamic-update-slice | bytes 1048580 | tf_op jit(solution)/shard_map/while/body/jit(dynamic_update_index_in_dim)/dynamic_update_slice | solution.py:191
  374.8 11.0 %dynamic_update_slice.29 = f32[4,512,1,256]{1,0,3,2:T(4,128)} dynamic-update-slice(f32[4,512,1,256]{1,0,3,2:T(4,128)} %get-tuple-element.390, f32[1,512,1,256]{1,0,3,2:T(1,128)S(1)} %copy.92, s32[]{:T(128)} %get-tuple-element.389, s32[]{:T(128)} %constant.83.clone.1..sunk, s32[]{:T(128)} %constant.83.clone.1..sunk, s32[]{:T(128)} %constant.83.clone.1..sunk) | dynamic-update-slice | bytes 1048580 | tf_op jit(solution)/shard_map/while/body/jit(dynamic_update_index_in_dim)/dynamic_update_slice | solution.py:191
  393.4 11.0 %dynamic_update_slice.30 = f32[4,512,1,256]{1,0,3,2:T(4,128)} dynamic-update-slice(f32[4,512,1,256]{1,0,3,2:T(4,128)} %get-tuple-element.391, f32[1,512,1,256]{1,0,3,2:T(1,128)S(1)} %copy.93, s32[]{:T(128)} %get-tuple-element.389, s32[]{:T(128)} %constant.83.clone.1..sunk, s32[]{:T(128)} %constant.83.clone.1..sunk, s32[]{:T(128)} %constant.83.clone.1..sunk) | dynamic-update-slice | bytes 1048580 | tf_op jit(solution)/shard_map/while/body/jit(dynamic_update_index_in_dim)/dynamic_update_slice | solution.py:191
  406.2 11.0 %dynamic_update_slice.29 = f32[4,512,1,256]{1,0,3,2:T(4,128)} dynamic-update-slice(f32[4,512,1,256]{1,0,3,2:T(4,128)} %get-tuple-element.390, f32[1,512,1,256]{1,0,3,2:T(1,128)S(1)} %copy.92, s32[]{:T(128)} %get-tuple-element.389, s32[]{:T(128)} %constant.83.clone.1..sunk, s32[]{:T(128)} %constant.83.clone.1..sunk, s32[]{:T(128)} %constant.83.clone.1..sunk) | dynamic-update-slice | bytes 1048580 | tf_op jit(solution)/shard_map/while/body/jit(dynamic_update_index_in_dim)/dynamic_update_slice | solution.py:191
  424.7 11.0 %dynamic_update_slice.30 = f32[4,512,1,256]{1,0,3,2:T(4,128)} dynamic-update-slice(f32[4,512,1,256]{1,0,3,2:T(4,128)} %get-tuple-element.391, f32[1,512,1,256]{1,0,3,2:T(1,128)S(1)} %copy.93, s32[]{:T(128)} %get-tuple-element.389, s32[]{:T(128)} %constant.83.clone.1..sunk, s32[]{:T(128)} %constant.83.clone.1..sunk, s32[]{:T(128)} %constant.83.clone.1..sunk) | dynamic-update-slice | bytes 1048580 | tf_op jit(solution)/shard_map/while/body/jit(dynamic_update_index_in_dim)/dynamic_update_slice | solution.py:191
  437.6 11.0 %dynamic_update_slice.29 = f32[4,512,1,256]{1,0,3,2:T(4,128)} dynamic-update-slice(f32[4,512,1,256]{1,0,3,2:T(4,128)} %get-tuple-element.390, f32[1,512,1,256]{1,0,3,2:T(1,128)S(1)} %copy.92, s32[]{:T(128)} %get-tuple-element.389, s32[]{:T(128)} %constant.83.clone.1..sunk, s32[]{:T(128)} %constant.83.clone.1..sunk, s32[]{:T(128)} %constant.83.clone.1..sunk) | dynamic-update-slice | bytes 1048580 | tf_op jit(solution)/shard_map/while/body/jit(dynamic_update_index_in_dim)/dynamic_update_slice | solution.py:191
  456.2 11.0 %dynamic_update_slice.30 = f32[4,512,1,256]{1,0,3,2:T(4,128)} dynamic-update-slice(f32[4,512,1,256]{1,0,3,2:T(4,128)} %get-tuple-element.391, f32[1,512,1,256]{1,0,3,2:T(1,128)S(1)} %copy.93, s32[]{:T(128)} %get-tuple-element.389, s32[]{:T(128)} %constant.83.clone.1..sunk, s32[]{:T(128)} %constant.83.clone.1..sunk, s32[]{:T(128)} %constant.83.clone.1..sunk) | dynamic-update-slice | bytes 1048580 | tf_op jit(solution)/shard_map/while/body/jit(dynamic_update_index_in_dim)/dynamic_update_slice | solution.py:191
  469.0 11.0 %dynamic_update_slice.29 = f32[4,512,1,256]{1,0,3,2:T(4,128)} dynamic-update-slice(f32[4,512,1,256]{1,0,3,2:T(4,128)} %get-tuple-element.390, f32[1,512,1,256]{1,0,3,2:T(1,128)S(1)} %copy.92, s32[]{:T(128)} %get-tuple-element.389, s32[]{:T(128)} %constant.83.clone.1..sunk, s32[]{:T(128)} %constant.83.clone.1..sunk, s32[]{:T(128)} %constant.83.clone.1..sunk) | dynamic-update-slice | bytes 1048580 | tf_op jit(solution)/shard_map/while/body/jit(dynamic_update_index_in_dim)/dynamic_update_slice | solution.py:191
  487.7 7.3 fusion.104
  506.6 5.2 add_convert_fusion
  513.6 4.3 fusion.124
  524.5 20.4 %all-reduce.25.cloned.1.call-done = (f32[640,256]{1,0:T(8,128)}, f32[640,256]{1,0:T(8,128)}) async-done(((f32[640,256]{1,0:T(8,128)}, f32[640,256]{1,0:T(8,128)}), (f32[640,256]{1,0:T(8,128)}, f32[640,256]{1,0:T(8,128)})) %all-reduce.25.cloned.1.call-update) | async-done | bytes 1310736 | tf_op jit(solution)/shard_map/psum | solution.py:315
  544.9 6.2 all-reduce.6
  551.1 56.0 %all-reduce.21.cloned.1.call-done = bf16[2048,640]{1,0:T(8,128)(2,1)} async-done(((bf16[2048,640]{1,0:T(8,128)(2,1)}), bf16[2048,640]{1,0:T(8,128)(2,1)}) %all-reduce.21.cloned.1.call-update) | async-done | bytes 2621456 | tf_op jit(solution)/shard_map/psum | solution.py:272
  607.1 4.0 fusion.56
  611.1 39.5 %all-reduce.4 = (f32[640]{0:T(1024)}, f32[256]{0:T(256)}, f32[256]{0:T(256)}, f32[640]{0:T(1024)}, f32[640]{0:T(1024)}, /*index=5*/f32[640]{0:T(1024)}) all-reduce(f32[640]{0:T(1024)S(1)} %get-tuple-element.152, f32[256]{0:T(256)S(1)} %get-tuple-element.205, ...), channel_id=1, replica_groups=mesh['dp'=8,'tensor'=4] {'dp'}, use_global_device_ids=true, to_apply=%region_33.34 | all-reduce | flops 3072 | bytes 24576 | tf_op jit(solution)/shard_map/psum | solution.py:330
  650.6 5.7 fusion.60
  656.3 182.4 %all-reduce.23.cloned.1.call-done = (f32[640,256]{1,0:T(8,128)}, f32[640,256]{1,0:T(8,128)}, f32[640,256]{1,0:T(8,128)}, f32[256,640]{1,0:T(8,128)}, f32[640,512...) async-done(((f32[640,256]{1,0:T(8,128)}, f32[640,256]{1,0:T(8,128)}, f32[640,256]{1,0:T(8,128)}, f32[256,640]{1,0:T(8,128)}, f32[640,512]{1,0:T(8,128)}, ...) | async-done | bytes 6553616 | tf_op jit(solution)/shard_map/psum | solution.py:330
  (310 shorter events, 156.5 us)
Async XLA Ops:
  7.2 188.2 %copy-start = (bf16[512,640]{1,0:T(8,128)(2,1)S(1)}, bf16[512,640]{1,0:T(8,128)(2,1)}, u32[]{:S(2)}) copy-start(bf16[512,640]{1,0:T(8,128)(2,1)} %param.28) | copy-start | bytes 1966084
  7.2 173.0 %all-reduce.15.cloned.1.call-start = ((), (), s32[]{:S(2)}) async-start(), calls=%async_computation | async-start | bytes 10485760 | tf_op jit(solution)/shard_map/psum | solution.py:263
  7.3 14.1 %copy-start.65 = (f32[128]{0:T(128)}, f32[128]{0:T(128)S(1)}, u32[]{:S(2)}) copy-start(f32[128]{0:T(128)S(1)} %multiply_power_fusion) | copy-start | bytes 1540
  10.8 4.7 copy-start.15
  13.2 5.4 copy-start.45
  15.5 5.8 copy-start.53
  15.6 5.7 copy-start.43
  35.6 3.7 copy-start.60
  74.8 184.1 %all-reduce.17.cloned.1.call-start = ((), (), s32[]{:S(2)}) async-start(), calls=%async_computation.1 | async-start | bytes 5242880 | tf_op jit(solution)/shard_map/psum | solution.py:266
  180.2 4.0 copy-start.2
  190.0 4.1 copy-start.69
  198.7 139.5 %all-reduce.19.cloned.1.call-start = ((), (), s32[]{:S(2)}) async-start(), calls=%async_computation.2 | async-start | bytes 5242880 | tf_op jit(solution)/shard_map/psum | solution.py:269
  261.5 4.2 copy-start.12
  261.5 5.7 copy-start.72
  267.1 5.6 copy-start.25
  267.8 4.9 copy-start.36
  278.1 266.8 %all-reduce.25.cloned.1.call-start = ((), (), s32[]{:S(2)}) async-start(), calls=%async_computation.5 | async-start | bytes 2621440 | tf_op jit(solution)/shard_map/psum | solution.py:315
  338.2 4.4 copy-start.13
  338.2 4.8 copy-start.18
  342.6 8.2 slice-start
  343.1 7.8 slice-start.1
  487.6 7.4 copy-start.8
  487.7 7.4 copy-start.46
  487.7 7.4 copy-start.58
  505.5 101.5 %all-reduce.21.cloned.1.call-start = ((), (), s32[]{:S(2)}) async-start(), calls=%async_computation.3 | async-start | bytes 5242880 | tf_op jit(solution)/shard_map/psum | solution.py:272
  511.9 326.8 %all-reduce.23.cloned.1.call-start = ((), (), s32[]{:S(2)}) async-start(), calls=%async_computation.4 | async-start | bytes 13107200 | tf_op jit(solution)/shard_map/psum | solution.py:330
  513.6 4.3 copy-start.20
  544.9 62.2 %copy-start.5 = (bf16[2048,640]{1,0:T(8,128)(2,1)S(1)}, bf16[2048,640]{1,0:T(8,128)(2,1)}, u32[]{:S(2)}) copy-start(bf16[2048,640]{1,0:T(8,128)(2,1)} %param.21) | copy-start | bytes 7864324
  551.1 99.5 %copy-start.50 = (f32[2048]{0:T(1024)S(1)}, f32[2048]{0:T(1024)}, u32[]{:S(2)}) copy-start(f32[2048]{0:T(1024)} %copy-done.49) | copy-start | bytes 24580
  838.7 4.1 copy-start.34
  838.7 4.9 copy-start.33
  838.7 5.8 copy-start.32
  (49 other events, 101.3 us)
Sparse Core Ops, SparseCore 0:
  74.9 105.2 all-reduce.14
  198.8 60.0 all-reduce.16
  278.2 59.9 all-reduce.18
  505.6 39.1 all-reduce.24
  547.1 59.9 all-reduce.20
  613.5 225.1 all-reduce.22
